TPU v7x, 768 devices: a whole 4x8x12 slice. The times are simulated.
768 devices in a mesh: segment: 48 (over x, z_lo, core), tensor: 16 (over z_hi, y).
Axes of the slice: x: 4, y: 8, z: 12 (z_hi: 2, z_lo: 6; z = z_hi * 6 + z_lo), core: 2. Of those that a mesh axis runs over, the one named last changes fastest.
Arguments:
- down_terms: bfloat16 [16, 6144, 8192], P('tensor', 'segment'), may hold values from -1.5 to 1.5
- residual: bfloat16 [6144, 8192], P(('segment', 'tensor'))
- norm_gain: bfloat16 [48, 8192], P('segment'), may hold values from 0.25 to 1.75
- key_value_weight: bfloat16 [48, 8192, 2048], P('segment', None, 'tensor'), may hold values from -0.0625 to 0.0625
- step_powers: int32 [3, 48, 64, 16], P(None, 'segment', None, 'tensor'), may hold values from -12 to -6, as said below
- bit_logits: float32 [80, 3], replicated, may hold values from -2 to 2
- layer_counts: int32 [48], replicated, may hold values from 1 to 4, 80 in all
Outputs:
- stream: bfloat16 [6144, 8192], P(('segment', 'tensor'))
- key_values: bfloat16 [6144, 2048], P('segment', 'tensor')
Inputs may be any that keep to these rules, and one draw needn't show every extreme that they name: `layer_counts`: the counts sum to 80 and the largest is exactly 4. `step_powers`: entries of the 2, 4 and 8 bit candidates (first index 0, 1, 2) lie in -8 to -6, -9 to -7 and -12 to -10.
All inputs are finite; a program needn't handle non-finite values.
Results may differ from a plain program's by a relative error of at most 0.018.
Values may be sent and summed in bfloat16 or wider, within the bound.
A program may use at most 32 MiB of HBM per device.

v0:
```python
import jax
import jax.numpy as jnp
from jax import lax
from jax.sharding import PartitionSpec as P

QTILE = 128


def passed_along(block, axis, distance):
    devices = range(lax.axis_size(axis))
    route = [((i - distance) % len(devices), i) for i in devices]
    return lax.ppermute(block, axis, route)


def step_sizes(powers):
    sizes = jnp.zeros(powers.shape, jnp.float32)
    for power in range(-12, -5):
        sizes = jnp.where(powers == power, 2.0**power, sizes)
    return sizes


def mix_weight(weight, powers, shares, tile):
    height, width = weight.shape
    values = weight.astype(jnp.float32).reshape(height // tile, tile, width // tile, tile)
    total = jnp.zeros_like(values)
    for which, bits in enumerate((2, 4, 8)):
        step = step_sizes(powers[which])[:, None, :, None]
        levels = jnp.clip(
            jnp.floor(values / step + 0.5), -(2.0 ** (bits - 1)), 2.0 ** (bits - 1) - 1.0
        )
        total = total + shares[which] * (levels * step)
    return total.reshape(height, width).astype(jnp.bfloat16)


def rms_scale(stream, gain):
    values = stream.astype(jnp.float32)
    mean_square = jnp.mean(values * values, axis=-1, keepdims=True)
    return (values * lax.rsqrt(mean_square + 1e-05) * gain.astype(jnp.float32)).astype(jnp.bfloat16)


def body(down_terms, residual, norm_gain, key_value_weight, step_powers, bit_logits, layer_counts):
    section = lax.axis_index("segment")
    sections = layer_counts.shape[0]
    before = lax.broadcasted_iota(jnp.int32, (sections,), 0) < section
    first = jnp.sum(jnp.where(before, layer_counts, 0))
    depth = bit_logits.shape[0]
    picked = lax.broadcasted_iota(jnp.int32, (depth, 1), 0) == first
    logit_row = jnp.sum(jnp.where(picked, bit_logits, 0.0), axis=0)
    raised = jnp.exp(logit_row)
    shares = raised / jnp.sum(raised)
    mixed = mix_weight(key_value_weight[0], step_powers[:, 0], shares, QTILE)
    share_rows = residual.shape[0]
    offset = lax.axis_index("tensor") * share_rows
    gain = norm_gain[0]
    whole_rows = None
    summed = lax.psum_scatter(
        down_terms[0].astype(jnp.float32).astype(jnp.bfloat16),
        "tensor",
        scatter_dimension=0,
        tiled=True,
    ).astype(jnp.float32)
    hidden = (summed + residual.astype(jnp.float32)).astype(jnp.bfloat16)
    gathered = lax.all_gather(hidden, "tensor", axis=0, tiled=True)
    arrived = passed_along(gathered, "segment", 1)
    normed = rms_scale(arrived, gain)
    key_values = jnp.dot(normed, mixed, preferred_element_type=jnp.float32).astype(jnp.bfloat16)
    stream = lax.dynamic_slice_in_dim(arrived, offset, share_rows, 0)
    return (stream, key_values)


def solution(mesh):
    return jax.shard_map(
        body,
        mesh=mesh,
        in_specs=(
            P("tensor", "segment", None),
            P(("segment", "tensor"), None),
            P("segment", None),
            P("segment", None, "tensor"),
            P(None, "segment", None, "tensor"),
            P(),
            P(),
        ),
        out_specs=(P(("segment", "tensor"), None), P("segment", "tensor")),
        check_vma=False,
    )
```

profile of v0, /device:TPU:6, one launch (start us, length us, event | category | flops | bytes accessed | tf_op | source)
XLA Modules:
  0.0 441.3 jit_solution(3793623520288192452)
XLA Ops:
  7.2 0.0 copy-start
  7.2 0.0 copy-start.1
  7.2 0.0 copy-start.5
  7.2 0.0 copy-start.2
  7.2 0.0 copy-start.3
  7.2 0.0 reduce-scatter.2.cloned.1.call-start
  7.3 0.7 reduce-scatter.2.cloned.1.call-update
  7.9 0.0 all-gather.2.cloned.1.call-start
  8.0 261.1 %reduce-scatter.2.cloned.1.call-done = bf16[8,8192]{1,0:T(8,128)(2,1)} async-done(((bf16[128,8192]{1,0:T(8,128)(2,1)}), bf16[8,8192]{1,0:T(8,128)(2,1)}) %reduce-scatter.2.cloned.1.call-update) | async-done | bytes 131088 | tf_op jit(solution)/shard_map/reduce_scatter | solution.py:56
  269.1 0.0 copy-done
  269.1 1.6 add_convert_fusion
  270.7 0.0 all-gather.2.cloned.1.call-update
  270.7 122.6 %all-gather.2.cloned.1.call-done = bf16[128,8192]{1,0:T(8,128)(2,1)} async-done(((bf16[8,8192]{1,0:T(8,128)(2,1)}), bf16[128,8192]{1,0:T(8,128)(2,1)}) %all-gather.2.cloned.1.call-update) | async-done | bytes 2097168 | tf_op jit(solution)/shard_map/all_gather | solution.py:63
  393.3 1.9 collective-permute-start
  395.2 0.0 copy-done.1
  395.3 0.0 copy-done.5
  395.3 0.0 copy-start.4
  395.3 0.6 fusion.44
  395.9 0.6 iota_compare_fusion
  396.6 0.0 copy-done.2
  396.6 0.1 select_reduce_fusion
  396.7 0.6 exponential_reduce_fusion
  397.3 0.6 exponential_divide_fusion
  398.0 0.6 fusion.55
  398.6 0.0 copy-done.3
  398.6 0.1 broadcast_bitcast_fusion.2
  398.7 0.1 broadcast_bitcast_fusion
  398.8 27.8 %collective-permute-done = bf16[128,8192]{1,0:T(8,128)(2,1)S(1)} collective-permute-done((bf16[128,8192]{1,0:T(8,128)(2,1)}, bf16[128,8192]{1,0:T(8,128)(2,1)S(1)}, u32[]{:S(2)}, u32[]{:S(2)}) %collective-permute-start) | collective-permute-done | bytes 2097184 | tf_op jit(solution)/shard_map/ppermute | solution.py:12
  426.5 0.5 fusion
  427.0 0.7 constant_dynamic-slice_fusion
  427.7 0.0 copy-done.4
  427.7 6.8 %fusion.39 = bf16[128,128]{1,0:T(8,128)(2,1)} fusion(bf16[1,8192,128]{2,1,0:T(8,128)(2,1)S(1)} %copy-done.4, f32[8192]{0:T(1024)S(1)} %get-tuple-element.8, f32[]{:T(128)} %bitcast.10, f32[8192]{0:T(1024)S(1)} %get-tuple-element.9, f32[]{:T(128)} %bitcast.6, f32[8192]{0:T(1024)S(1)} %broadcast_bitcast_fusion.2, f32[]{:T(128)} %bitcast.2, ...), kind=kOutput, calls=%fused_computation.42 | convolution fusion | flops 295714816 | bytes 4358668 | tf_op jit(solution)/shard_map/dot_general | solution.py:66
  (3 shorter events, 0.1 us)
Async XLA Ops:
  7.2 261.9 %copy-start = (bf16[8,8192]{1,0:T(8,128)(2,1)S(1)}, bf16[8,8192]{1,0:T(8,128)(2,1)}, u32[]{:S(2)}) copy-start(bf16[8,8192]{1,0:T(8,128)(2,1)} %param.8) | copy-start | bytes 393220
  7.2 388.0 %copy-start.1 = (bf16[1,8192]{1,0:T(2,128)(2,1)S(1)}, bf16[1,8192]{1,0:T(2,128)(2,1)}, u32[]{:S(2)}) copy-start(bf16[1,8192]{1,0:T(2,128)(2,1)} %param.9) | copy-start | bytes 49156
  7.2 388.1 %copy-start.5 = (s32[48]{0:T(128)S(1)}, s32[48]{0:T(128)}, u32[]{:S(2)}) copy-start(s32[48]{0:T(128)} %param.13) | copy-start | bytes 580
  7.2 389.4 %copy-start.2 = (f32[80,3]{0,1:T(4,128)S(1)}, f32[80,3]{0,1:T(4,128)}, u32[]{:S(2)}) copy-start(f32[80,3]{0,1:T(4,128)} %param.12) | copy-start | bytes 2884
  7.2 391.4 %copy-start.3 = (s32[3,1,64,1]{2,3,1,0:T(1,128)S(1)}, s32[3,1,64,1]{2,3,1,0:T(1,128)}, u32[]{:S(2)}) copy-start(s32[3,1,64,1]{2,3,1,0:T(1,128)} %param.11) | copy-start | bytes 2308
  7.2 261.9 %reduce-scatter.2.cloned.1.call-start = ((), (), s32[]{:S(2)}) async-start(), calls=%async_computation.1 | async-start | bytes 2228224 | tf_op jit(solution)/shard_map/reduce_scatter | solution.py:56
  7.9 385.3 %all-gather.2.cloned.1.call-start = ((), (), s32[]{:S(2)}) async-start(), calls=%async_computation.2 | async-start | bytes 2228224 | tf_op jit(solution)/shard_map/all_gather | solution.py:63
  393.3 33.3 %collective-permute-start = (bf16[128,8192]{1,0:T(8,128)(2,1)}, bf16[128,8192]{1,0:T(8,128)(2,1)S(1)}, u32[]{:S(2)}, u32[]{:S(2)}) collective-permute-start(bf16[128,8192]{1,0:T(8,128)(2,1)} %all-gather.2.cloned.1.call-done), channel_id=1, source_target_pairs={{752,0},{0,16},{16,32},{32,48},{48,64},{64,80},{80,96},{96,112},{1... | collective-permute-start | bytes 6291464 | tf_op jit(solution)/shard_map/ppermute | solution.py:12
  395.3 32.4 %copy-start.4 = (bf16[1,8192,128]{2,1,0:T(8,128)(2,1)S(1)}, bf16[1,8192,128]{2,1,0:T(8,128)(2,1)}, u32[]{:S(2)}) copy-start(bf16[1,8192,128]{2,1,0:T(8,128)(2,1)} %param.10) | copy-start | bytes 6291460
Sparse Core Ops, SparseCore 0:
  13.2 255.8 reduce-scatter.1
  274.1 119.1 all-gather.1
where the time goes:
time: 442 us; the launch traced here: 441 us
  waiting for transfers between devices  412 us (93%)
  between operations  14.2 us (3%)
  matrix products  6.77 us (2%)
  other arithmetic  4.79 us (1%)
    reduce_scatter x1, waiting for transfers between devices, body(): lax.psum_scatter(down_terms[0].astype(jnp.float32).astype(jnp.bfloat16),...  261 us
    all_gather x1, waiting for transfers between devices, body(): gathered = lax.all_gather(hidden, 'tensor', axis=0, tiled=True)  123 us
    ppermute x1, waiting for transfers between devices, passed_along(): return lax.ppermute(block, axis, route)  27.8 us
  transfers between devices with their start and end apart: 3, of which 3 were waited for; matrix products, arithmetic and copies ran while one was open for 1% of the time, Pallas kernels for 0%

commit v1 on v0

v1 whole, which is shorter than its diff:
```python
import jax
import jax.numpy as jnp
from jax import lax
from jax.experimental import pallas as pl
from jax.experimental.pallas import tpu as pltpu
from jax.sharding import PartitionSpec as P

MESH = pl.DeviceIdType.MESH
QTILE = 128
RING = 8
CHUNKS = 8
BLOCK = 16
LIMIT = 1e30
BITS = (2, 4, 8)
LOWEST = (-8, -9, -12)


def hops(direction, chunk):
    return 4 if (chunk + direction) % 2 == 0 else 3


def schedule(chunks, stagger=0.6, step=1.0, cross=4.0):
    steps = []
    for c in range(chunks):
        begin = stagger * c
        for s in range(1, 5):
            steps.append((begin + step * (s - 1), 0, ("reduce", c, s)))
        done = begin + step * 4
        steps.append((done, 0, ("finish", c, 0)))
        steps.append((done + cross, 1, ("hidden", c, 0)))
        for s in range(1, 4):
            steps.append((done + cross + step * s, 1, ("gather", c, s)))
        steps.append((done + cross + step * 4.5, 2, ("product", c, 0)))
        steps.append((1.5 + 0.7 * c, 3, ("mix", c, 0)))
    steps.sort(key=lambda item: item[:2])
    return [item[2] for item in steps]


def kernel(
    powers, logits, counts, terms_hbm, residual_hbm, gain, weight_hbm,
    stream, key_values,
    terms, residual, weight, mixed, arrived, partial, crossed, gathered, scaled, total, squares,
    load_sem, reduce_send, reduce_recv, cross_send, cross_recv, gather_send, gather_recv,
):
    f32, bf16 = jnp.float32, jnp.bfloat16
    section, sections = lax.axis_index("segment"), lax.axis_size("segment")
    t = lax.axis_index("tensor")
    y, z = lax.rem(t, RING), lax.div(t, RING)
    ring = z * RING
    neighbour = (ring + lax.rem(y + 1, RING), ring + lax.rem(y + RING - 1, RING))
    far = lax.rem(t + RING, 2 * RING)
    after, before = lax.rem(section + 1, sections), lax.rem(section + sections - 1, sections)
    depth = terms.shape[1]
    width = depth // CHUNKS

    def columns(c):
        return pl.ds(c * width, width)

    def rows(d):
        return pl.ds(pl.multiple_of(lax.rem(d + 2 * RING, RING) * BLOCK, BLOCK), BLOCK)

    def offset(direction, distance):
        return y + distance if direction == 0 else y - distance

    loads = [
        pltpu.make_async_copy(residual_hbm, residual, load_sem.at[0]),
        pltpu.make_async_copy(terms_hbm, terms, load_sem.at[1]),
        pltpu.make_async_copy(weight_hbm, weight, load_sem.at[2]),
    ]
    for load in loads:
        load.start()

    barrier = pltpu.get_barrier_semaphore()
    for there in (neighbour[0], neighbour[1]):
        pl.semaphore_signal(barrier, inc=1, device_id=(section, there), device_id_type=MESH)
    for there in (t, far):
        pl.semaphore_signal(barrier, inc=1, device_id=(before, there), device_id_type=MESH)

    first = jnp.int32(0)
    for q in range(sections):
        first = first + jnp.where(q < section, counts[q], 0)
    raised = [jnp.exp(jnp.full((8, 128), logits[first, b], f32)) for b in range(3)]
    whole = raised[0] + raised[1] + raised[2]
    shares = [(r / whole)[0:1, :] for r in raised]

    loads[0].wait()
    loads[1].wait()
    own = pl.ds(pl.multiple_of(lax.div(t, 2) * BLOCK, BLOCK), BLOCK)
    half = lax.rem(t, 2)
    row = lax.broadcasted_iota(jnp.int32, (BLOCK, width), 0)
    mine = lax.div(row, 8) == half
    for c in range(CHUNKS):
        extra = residual[:, columns(c)].astype(f32)
        extra = jnp.where(mine, jnp.concatenate([extra, extra], axis=0), 0.0)
        terms[own, columns(c)] = (terms[own, columns(c)].astype(f32) + extra).astype(bf16)

    pl.semaphore_wait(barrier, 4)

    sent = []

    def send(src, dst, send_sem, recv_sem, there):
        copy = pltpu.make_async_remote_copy(
            src_ref=src, dst_ref=dst, send_sem=send_sem, recv_sem=recv_sem,
            device_id=there, device_id_type=MESH,
        )
        copy.start()
        sent.append(copy)

    def receive(dst, recv_sem):
        pltpu.make_async_remote_copy(
            src_ref=dst, dst_ref=dst, send_sem=recv_sem, recv_sem=recv_sem,
            device_id=(section, neighbour[0]), device_id_type=MESH,
        ).wait_recv()

    def reduce(c, s):
        for direction in range(2):
            length = hops(direction, c)
            if s > length:
                continue
            d = rows(offset(direction, length + 1 - s))
            if s == 1:
                src = terms.at[d, columns(c)]
            else:
                src = arrived.at[direction, s - 2, :, columns(c)]
                receive(src, reduce_recv.at[direction, s - 2, c])
                src[...] = (src[...].astype(f32) + terms[d, columns(c)].astype(f32)).astype(bf16)
            send(
                src,
                arrived.at[direction, s - 1, :, columns(c)],
                reduce_send.at[direction, s - 1, c],
                reduce_recv.at[direction, s - 1, c],
                (section, neighbour[direction]),
            )

    def finish(c, s):
        value = terms[rows(y), columns(c)].astype(f32)
        for direction in (1, 0) if hops(0, c) == 4 else (0, 1):
            last = hops(direction, c) - 1
            src = arrived.at[direction, last, :, columns(c)]
            receive(src, reduce_recv.at[direction, last, c])
            value = value + src[...].astype(f32)
        partial[:, columns(c)] = value.astype(bf16)
        for slot, there in ((1, far), (0, t)):
            send(
                partial.at[:, columns(c)],
                crossed.at[slot, :, columns(c)],
                cross_send.at[slot, c],
                cross_recv.at[slot, c],
                (after, there),
            )

    def pass_on(c, s, d):
        for direction in range(2):
            if s > hops(direction, c):
                continue
            block = gathered.at[rows(offset(direction, -(s - 1))), columns(c)]
            if s > 1:
                receive(block, gather_recv.at[direction, s - 2, c])
            send(
                block, block, gather_send.at[direction, s - 1, c], gather_recv.at[direction, s - 1, c],
                (section, neighbour[direction]),
            )

    def hidden(c, s):
        for slot in range(2):
            receive(crossed.at[slot, :, columns(c)], cross_recv.at[slot, c])
        value = crossed[0, :, columns(c)].astype(f32) + crossed[1, :, columns(c)].astype(f32)
        gathered[rows(y), columns(c)] = value.astype(bf16)
        pass_on(c, 1, None)

    def gather(c, s):
        pass_on(c, s + 1, None)

    def product(c, s):
        for direction in range(2):
            last = hops(direction, c)
            block = gathered.at[rows(offset(direction, -last)), columns(c)]
            receive(block, gather_recv.at[direction, last - 1, c])
        piece = 256
        for j in range(width // piece):
            at = pl.ds(c * width + j * piece, piece)
            values = gathered[:, at].astype(f32)
            square = values * values
            square = square[:, :128] + square[:, 128:]
            if c == first_product and j == 0:
                squares[...] = square
            else:
                squares[...] += square
            values = jnp.clip(values * gain[0:1, at].astype(f32), -LIMIT, LIMIT)
            scaled[:, pl.ds(j * piece, piece)] = values.astype(bf16)
        result = jnp.dot(scaled[...], mixed[columns(c), :], preferred_element_type=f32)
        if c == first_product:
            total[...] = result
        else:
            total[...] += result
        block = gathered[own, columns(c)].astype(f32)
        stream[:, columns(c)] = jnp.where(half == 0, block[:8], block[8:]).astype(bf16)

    def mix(c, s):
        if c == 0:
            loads[2].wait()
        tiles = width // QTILE

        def one(i, carry):
            tile = c * tiles + i
            at = pl.ds(pl.multiple_of(tile * QTILE, QTILE), QTILE)
            values = weight[at, :].astype(f32)
            result = None
            for b, bits in enumerate(BITS):
                power, low = powers[b * (depth // QTILE) + tile], LOWEST[b]
                step = jnp.where(power == low, 2.0**low, jnp.where(power == low + 1, 2.0 ** (low + 1), 2.0 ** (low + 2)))
                inverse = jnp.where(power == low, 2.0**-low, jnp.where(power == low + 1, 2.0 ** (-low - 1), 2.0 ** (-low - 2)))
                levels = jnp.clip(jnp.floor(values * inverse + 0.5), -(2.0 ** (bits - 1)), 2.0 ** (bits - 1) - 1.0)
                part = levels * (shares[b] * step)
                result = part if result is None else result + part
            mixed[at, :] = result.astype(bf16)
            return carry

        lax.fori_loop(0, tiles, one, 0)

    order = schedule(CHUNKS)
    first_product = [c for name, c, s in order if name == "product"][0]
    act = dict(reduce=reduce, finish=finish, hidden=hidden, gather=gather, product=product, mix=mix)
    for name, c, s in order:
        act[name](c, s)

    mean = jnp.sum(squares[...], axis=1, keepdims=True) * (1.0 / depth)
    key_values[...] = (total[...] * lax.rsqrt(mean + 1e-05)).astype(bf16)
    for copy in sent:
        copy.wait_send()


def body(down_terms, residual, norm_gain, key_value_weight, step_powers, bit_logits, layer_counts):
    terms, weight = down_terms[0], key_value_weight[0]
    depth, wide = weight.shape
    bf16, f32 = jnp.bfloat16, jnp.float32
    vmem, smem, anywhere = pltpu.VMEM, pltpu.SMEM, pl.ANY
    dma = pltpu.SemaphoreType.DMA
    return pl.pallas_call(
        kernel,
        out_shape=(
            jax.ShapeDtypeStruct(residual.shape, bf16),
            jax.ShapeDtypeStruct((terms.shape[0], wide), bf16),
        ),
        in_specs=[
            pl.BlockSpec(memory_space=smem),
            pl.BlockSpec(memory_space=smem),
            pl.BlockSpec(memory_space=smem),
            pl.BlockSpec(memory_space=anywhere),
            pl.BlockSpec(memory_space=anywhere),
            pl.BlockSpec(memory_space=vmem),
            pl.BlockSpec(memory_space=anywhere),
        ],
        out_specs=(pl.BlockSpec(memory_space=vmem), pl.BlockSpec(memory_space=vmem)),
        scratch_shapes=[
            vmem(terms.shape, bf16),
            vmem(residual.shape, bf16),
            vmem(weight.shape, bf16),
            vmem(weight.shape, bf16),
            vmem((2, 4, BLOCK, depth), bf16),
            vmem((BLOCK, depth), bf16),
            vmem((2, BLOCK, depth), bf16),
            vmem(terms.shape, bf16),
            vmem((terms.shape[0], depth // CHUNKS), bf16),
            vmem((terms.shape[0], wide), f32),
            vmem((terms.shape[0], 128), f32),
            dma((3,)),
            dma((2, 4, CHUNKS)),
            dma((2, 4, CHUNKS)),
            dma((2, CHUNKS)),
            dma((2, CHUNKS)),
            dma((2, 4, CHUNKS)),
            dma((2, 4, CHUNKS)),
        ],
        compiler_params=pltpu.CompilerParams(
            collective_id=0, has_side_effects=True, vmem_limit_bytes=56 << 20
        ),
    )(
        step_powers.reshape(-1), bit_logits, layer_counts, terms, residual, norm_gain, weight,
    )


def solution(mesh):
    return jax.shard_map(
        body,
        mesh=mesh,
        in_specs=(
            P("tensor", "segment", None),
            P(("segment", "tensor"), None),
            P("segment", None),
            P("segment", None, "tensor"),
            P(None, "segment", None, "tensor"),
            P(),
            P(),
        ),
        out_specs=(P(("segment", "tensor"), None), P("segment", "tensor")),
        check_vma=False,
    )
```

time: 442 us -> 83.1 us (0.19)
  waiting for transfers between devices: 412 us -> 0 us
  Pallas kernels: 0 us -> 76.4 us
  between operations: 14.2 us -> 0.64 us
  matrix products: 6.77 us -> 0 us
    reduce_scatter x1 -> x0, waiting for transfers between devices: 261 us -> none  [body(): lax.psum_scatter(down_terms[0].astype(jnp.float32).astype(jnp.bfloat16),...]
    all_gather x1 -> x0, waiting for transfers between devices: 123 us -> none  [body(): gathered = lax.all_gather(hidden, 'tensor', axis=0, tiled=True)]
    pallas_call x0 -> x1, Pallas kernels: none -> 76.4 us  [body(): pl.pallas_call(kernel, out_shape=(jax.ShapeDtypeStruct(residual.shape, bf...]
    ppermute x1 -> x0, waiting for transfers between devices: 27.8 us -> none  [passed_along(): return lax.ppermute(block, axis, route)]
    dot_general x1 -> x0, matrix products: 6.77 us -> none  [body(): jnp.dot(normed, mixed, preferred_element_type=jnp.float32)]
  transfers between devices with their start and end apart: 3 -> 0, of which waited for: 3 -> 0; matrix products, arithmetic and copies ran while one was open for 1% -> 0% of each run, Pallas kernels for 0% -> 0%
where the time goes in v1:
time: 83.1 us; the launch traced here: 82.7 us
  Pallas kernels  76.4 us (92%)
  local copies, waits for them, and re-layouts  4.98 us (6%)
    pallas_call x1, Pallas kernels, body(): pl.pallas_call(kernel, out_shape=(jax.ShapeDtypeStruct(residual.shape, bf...  76.4 us
    unnamed x3, local copies, waits for them, and re-layouts  4.33 us

profile of v1, /device:TPU:6, one launch (start us, length us, event | category | flops | bytes accessed | tf_op | source)
XLA Modules:
  0.0 82.7 jit_solution(1552347174786641124)
XLA Ops:
  0.6 0.7 reduce
  1.3 0.6 reshape.7.powers
  2.0 1.4 %copy.9.logits = f32[80,3]{1,0:T(8,128)} copy(f32[80,3]{0,1:T(4,128)} %param.12) | data formatting | bytes 1920 | tf_op args[5]
  3.4 76.4 %shard_map.86 = (bf16[8,8192]{1,0:T(8,128)(2,1)}, bf16[128,128]{1,0:T(8,128)(2,1)}) custom-call(s32[192]{0:T(256)} %reshape.7.powers, f32[80,3]{1,0:T(8,128)} %copy.9.logits, s32[48]{0:T(128)} %counts.1, bf16[128,8192]{1,0:T(8,128)(2,1)} %bitcast.2, bf16[8,8192]{1,0:T(8,128)(2,1)} %residual_hbm.1, bf16[1,8192]{1,0:T(2,128)(2,1)} %gain.1, ...), custom_call_target="tpu_custom_call" | custom-call | tf_op jit(solution)/shard_map/pallas_call | solution.py:239
  79.8 1.6 %copy.12 = bf16[8,8192]{1,0:T(8,128)(2,1)} copy(bf16[8,8192]{1,0:T(8,128)(2,1)} %get-tuple-element.4) | data formatting | bytes 262144
  81.4 1.4 %copy.13 = bf16[128,128]{1,0:T(8,128)(2,1)} copy(bf16[128,128]{1,0:T(8,128)(2,1)} %get-tuple-element.5) | data formatting | bytes 65536

commit v2 on v1

--- a/solution.py
+++ b/solution.py
@@ -8,9 +8,12 @@
 MESH = pl.DeviceIdType.MESH
 QTILE = 128
 RING = 8
-CHUNKS = 8
+SIZES = (2048,) * 4
+CHUNKS = len(SIZES)
+STAGGER, STEP, CROSS = 0.6, 1.0, 4.0
 BLOCK = 16
 LIMIT = 1e30
+FIRST = 3
 BITS = (2, 4, 8)
 LOWEST = (-8, -9, -12)
 
@@ -19,7 +22,7 @@
     return 4 if (chunk + direction) % 2 == 0 else 3
 
 
-def schedule(chunks, stagger=0.6, step=1.0, cross=4.0):
+def schedule(chunks, stagger=STAGGER, step=STEP, cross=CROSS):
     steps = []
     for c in range(chunks):
         begin = stagger * c
@@ -37,10 +40,11 @@
 
 
 def kernel(
-    powers, logits, counts, terms_hbm, residual_hbm, gain, weight_hbm,
+    powers_hbm, logits_hbm, counts_hbm, terms_hbm, residual_hbm, gain_hbm, weight_hbm,
     stream, key_values,
+    powers, logits, counts, gain, taken, product_out,
     terms, residual, weight, mixed, arrived, partial, crossed, gathered, scaled, total, squares,
-    load_sem, reduce_send, reduce_recv, cross_send, cross_recv, gather_send, gather_recv,
+    load_sem, term_sem, store_sem, reduce_send, reduce_recv, cross_send, cross_recv, gather_send, gather_recv,
 ):
     f32, bf16 = jnp.float32, jnp.bfloat16
     section, sections = lax.axis_index("segment"), lax.axis_size("segment")
@@ -51,24 +55,16 @@
     far = lax.rem(t + RING, 2 * RING)
     after, before = lax.rem(section + 1, sections), lax.rem(section + sections - 1, sections)
     depth = terms.shape[1]
-    width = depth // CHUNKS
+    starts = [sum(SIZES[:c]) for c in range(CHUNKS)]
 
     def columns(c):
-        return pl.ds(c * width, width)
+        return pl.ds(starts[c], SIZES[c])
 
     def rows(d):
         return pl.ds(pl.multiple_of(lax.rem(d + 2 * RING, RING) * BLOCK, BLOCK), BLOCK)
 
     def offset(direction, distance):
         return y + distance if direction == 0 else y - distance
-
-    loads = [
-        pltpu.make_async_copy(residual_hbm, residual, load_sem.at[0]),
-        pltpu.make_async_copy(terms_hbm, terms, load_sem.at[1]),
-        pltpu.make_async_copy(weight_hbm, weight, load_sem.at[2]),
-    ]
-    for load in loads:
-        load.start()
 
     barrier = pltpu.get_barrier_semaphore()
     for there in (neighbour[0], neighbour[1]):
@@ -76,27 +72,33 @@
     for there in (t, far):
         pl.semaphore_signal(barrier, inc=1, device_id=(before, there), device_id_type=MESH)
 
-    first = jnp.int32(0)
-    for q in range(sections):
-        first = first + jnp.where(q < section, counts[q], 0)
-    raised = [jnp.exp(jnp.full((8, 128), logits[first, b], f32)) for b in range(3)]
-    whole = raised[0] + raised[1] + raised[2]
-    shares = [(r / whole)[0:1, :] for r in raised]
+    loads = [
+        pltpu.make_async_copy(src, dst, load_sem.at[i])
+        for i, (src, dst) in enumerate((
+            (residual_hbm, residual), (counts_hbm, counts), (logits_hbm, logits),
+            (powers_hbm, powers), (weight_hbm, weight), (gain_hbm, gain),
+        ))
+    ]
+    term_loads = [
+        pltpu.make_async_copy(terms_hbm.at[:, columns(c)], terms.at[:, columns(c)], term_sem.at[c])
+        for c in range(CHUNKS)
+    ]
+    loads[0].start()
+    for load in term_loads + loads[1:]:
+        load.start()
 
     loads[0].wait()
-    loads[1].wait()
     own = pl.ds(pl.multiple_of(lax.div(t, 2) * BLOCK, BLOCK), BLOCK)
     half = lax.rem(t, 2)
-    row = lax.broadcasted_iota(jnp.int32, (BLOCK, width), 0)
-    mine = lax.div(row, 8) == half
-    for c in range(CHUNKS):
+
+    def join(c, s):
+        term_loads[c].wait()
         extra = residual[:, columns(c)].astype(f32)
+        mine = lax.div(lax.broadcasted_iota(jnp.int32, (BLOCK, SIZES[c]), 0), 8) == half
         extra = jnp.where(mine, jnp.concatenate([extra, extra], axis=0), 0.0)
         terms[own, columns(c)] = (terms[own, columns(c)].astype(f32) + extra).astype(bf16)
 
-    pl.semaphore_wait(barrier, 4)
-
-    sent = []
+    sent, stores = [], []
 
     def send(src, dst, send_sem, recv_sem, there):
         copy = pltpu.make_async_remote_copy(
@@ -177,8 +179,8 @@
             block = gathered.at[rows(offset(direction, -last)), columns(c)]
             receive(block, gather_recv.at[direction, last - 1, c])
         piece = 256
-        for j in range(width // piece):
-            at = pl.ds(c * width + j * piece, piece)
+        for j in range(SIZES[c] // piece):
+            at = pl.ds(starts[c] + j * piece, piece)
             values = gathered[:, at].astype(f32)
             square = values * values
             square = square[:, :128] + square[:, 128:]
@@ -188,26 +190,26 @@
                 squares[...] += square
             values = jnp.clip(values * gain[0:1, at].astype(f32), -LIMIT, LIMIT)
             scaled[:, pl.ds(j * piece, piece)] = values.astype(bf16)
-        result = jnp.dot(scaled[...], mixed[columns(c), :], preferred_element_type=f32)
+        result = jnp.dot(scaled[:, : SIZES[c]], mixed[columns(c), :], preferred_element_type=f32)
         if c == first_product:
             total[...] = result
         else:
             total[...] += result
         block = gathered[own, columns(c)].astype(f32)
-        stream[:, columns(c)] = jnp.where(half == 0, block[:8], block[8:]).astype(bf16)
+        taken[:, columns(c)] = jnp.where(half == 0, block[:8], block[8:]).astype(bf16)
+        stores.append(pltpu.make_async_copy(taken.at[:, columns(c)], stream.at[:, columns(c)], store_sem.at[c]))
+        stores[-1].start()
 
     def mix(c, s):
-        if c == 0:
-            loads[2].wait()
-        tiles = width // QTILE
+        tiles = SIZES[c] // QTILE
 
         def one(i, carry):
-            tile = c * tiles + i
+            tile = starts[c] // QTILE + i
             at = pl.ds(pl.multiple_of(tile * QTILE, QTILE), QTILE)
             values = weight[at, :].astype(f32)
             result = None
             for b, bits in enumerate(BITS):
-                power, low = powers[b * (depth // QTILE) + tile], LOWEST[b]
+                power, low = powers[b, 0, 0, tile], LOWEST[b]
                 step = jnp.where(power == low, 2.0**low, jnp.where(power == low + 1, 2.0 ** (low + 1), 2.0 ** (low + 2)))
                 inverse = jnp.where(power == low, 2.0**-low, jnp.where(power == low + 1, 2.0 ** (-low - 1), 2.0 ** (-low - 2)))
                 levels = jnp.clip(jnp.floor(values * inverse + 0.5), -(2.0 ** (bits - 1)), 2.0 ** (bits - 1) - 1.0)
@@ -218,16 +220,41 @@
 
         lax.fori_loop(0, tiles, one, 0)
 
-    order = schedule(CHUNKS)
+    join(0, 0)
+    pl.semaphore_wait(barrier, 4)
+    reduce(0, 1)
+    for c in range(1, CHUNKS):
+        join(c, 0)
+        if c < FIRST:
+            reduce(c, 1)
+    for load in loads[1:]:
+        load.wait()
+    first = jnp.int32(0)
+    for q in range(sections):
+        first = first + jnp.where(q < section, counts[q], 0)
+    raised = [jnp.exp(jnp.full((8, 128), logits[b, first], f32)) for b in range(3)]
+    whole = raised[0] + raised[1] + raised[2]
+    shares = [(r / whole)[0:1, :] for r in raised]
+
+    order = [x for x in schedule(CHUNKS) if x[0] != "reduce" or x[2] > 1 or x[1] >= FIRST]
     first_product = [c for name, c, s in order if name == "product"][0]
     act = dict(reduce=reduce, finish=finish, hidden=hidden, gather=gather, product=product, mix=mix)
     for name, c, s in order:
         act[name](c, s)
 
     mean = jnp.sum(squares[...], axis=1, keepdims=True) * (1.0 / depth)
-    key_values[...] = (total[...] * lax.rsqrt(mean + 1e-05)).astype(bf16)
+    product_out[...] = (total[...] * lax.rsqrt(mean + 1e-05)).astype(bf16)
+    stores.append(pltpu.make_async_copy(product_out, key_values, store_sem.at[CHUNKS]))
+    stores[-1].start()
     for copy in sent:
         copy.wait_send()
+    for copy in stores:
+        copy.wait()
+
+
+def hand_out(stream_in, product_in, stream, key_values):
+    stream[...] = stream_in[...]
+    key_values[...] = product_in[...]
 
 
 def body(down_terms, residual, norm_gain, key_value_weight, step_powers, bit_logits, layer_counts):
@@ -236,23 +263,24 @@
     bf16, f32 = jnp.bfloat16, jnp.float32
     vmem, smem, anywhere = pltpu.VMEM, pltpu.SMEM, pl.ANY
     dma = pltpu.SemaphoreType.DMA
-    return pl.pallas_call(
+    out_shape = (
+        jax.ShapeDtypeStruct(residual.shape, bf16),
+        jax.ShapeDtypeStruct((terms.shape[0], wide), bf16),
+    )
+    powers = jnp.swapaxes(step_powers, 2, 3)
+    logits = bit_logits.T
+    outs = pl.pallas_call(
         kernel,
-        out_shape=(
-            jax.ShapeDtypeStruct(residual.shape, bf16),
-            jax.ShapeDtypeStruct((terms.shape[0], wide), bf16),
-        ),
-        in_specs=[
-            pl.BlockSpec(memory_space=smem),
-            pl.BlockSpec(memory_space=smem),
-            pl.BlockSpec(memory_space=smem),
-            pl.BlockSpec(memory_space=anywhere),
-            pl.BlockSpec(memory_space=anywhere),
-            pl.BlockSpec(memory_space=vmem),
-            pl.BlockSpec(memory_space=anywhere),
-        ],
-        out_specs=(pl.BlockSpec(memory_space=vmem), pl.BlockSpec(memory_space=vmem)),
+        out_shape=out_shape,
+        in_specs=[pl.BlockSpec(memory_space=anywhere)] * 7,
+        out_specs=(pl.BlockSpec(memory_space=anywhere),) * 2,
         scratch_shapes=[
+            smem(powers.shape, jnp.int32),
+            smem(logits.shape, f32),
+            smem(layer_counts.shape, jnp.int32),
+            vmem(norm_gain.shape, bf16),
+            vmem(residual.shape, bf16),
+            vmem((terms.shape[0], wide), bf16),
             vmem(terms.shape, bf16),
             vmem(residual.shape, bf16),
             vmem(weight.shape, bf16),
@@ -261,10 +289,12 @@
             vmem((BLOCK, depth), bf16),
             vmem((2, BLOCK, depth), bf16),
             vmem(terms.shape, bf16),
-            vmem((terms.shape[0], depth // CHUNKS), bf16),
+            vmem((terms.shape[0], max(SIZES)), bf16),
             vmem((terms.shape[0], wide), f32),
             vmem((terms.shape[0], 128), f32),
-            dma((3,)),
+            dma((6,)),
+            dma((CHUNKS,)),
+            dma((CHUNKS + 1,)),
             dma((2, 4, CHUNKS)),
             dma((2, 4, CHUNKS)),
             dma((2, CHUNKS)),
@@ -275,9 +305,14 @@
         compiler_params=pltpu.CompilerParams(
             collective_id=0, has_side_effects=True, vmem_limit_bytes=56 << 20
         ),
-    )(
-        step_powers.reshape(-1), bit_logits, layer_counts, terms, residual, norm_gain, weight,
-    )
+    )(powers, logits, layer_counts, terms, residual, norm_gain, weight)
+    return pl.pallas_call(
+        hand_out,
+        out_shape=out_shape,
+        in_specs=[pl.BlockSpec(memory_space=vmem)] * 2,
+        out_specs=(pl.BlockSpec(memory_space=vmem),) * 2,
+        compiler_params=pltpu.CompilerParams(vmem_limit_bytes=56 << 20),
+    )(*outs)
 
 
 def solution(mesh):

time: 83.1 us -> 76.6 us (0.922)
  the two profiles are of different devices: /device:TPU:6 before, /device:TPU:69 now
where the time goes in v2:
time: 76.6 us; the launch traced here: 76.4 us
  Pallas kernels  75.8 us (99%)
    pallas_call x1, Pallas kernels, body(): pl.pallas_call(kernel, out_shape=out_shape, in_specs=[pl.BlockSpec(memory...  74.2 us
    pallas_call x1, Pallas kernels, body(): pl.pallas_call(hand_out, out_shape=out_shape, in_specs=[pl.BlockSpec(memo...  1.57 us

profile of v2, /device:TPU:69, one launch (start us, length us, event | category | flops | bytes accessed | tf_op | source)
XLA Modules:
  0.0 76.4 jit_solution(4310221363679176819)
XLA Ops:
  0.6 74.2 %shard_map.86 = (bf16[8,8192]{1,0:T(8,128)(2,1)}, bf16[128,128]{1,0:T(8,128)(2,1)}) custom-call(s32[3,1,1,64]{3,2,1,0:T(1,128)} %bitcast.7, f32[3,80]{1,0:T(4,128)} %bitcast.6, s32[48]{0:T(128)} %counts_hbm.1, bf16[128,8192]{1,0:T(8,128)(2,1)} %bitcast.4, bf16[8,8192]{1,0:T(8,128)(2,1)} %residual_hbm.1, bf16[1,8192]{1,0:T(2,128)(2,1)} %gain_hbm.1, ...), custom_call_target="tpu_custom_call" | custom-call | tf_op jit(solution)/shard_map/pallas_call | solution.py:272
  74.8 1.6 %shard_map.87 = (bf16[8,8192]{1,0:T(8,128)(2,1)}, bf16[128,128]{1,0:T(8,128)(2,1)}) custom-call(bf16[8,8192]{1,0:T(8,128)(2,1)} %get-tuple-element.4.stream_in, bf16[128,128]{1,0:T(8,128)(2,1)} %get-tuple-element.5.product_in), custom_call_target="tpu_custom_call" | custom-call | tf_op jit(solution)/shard_map/pallas_call | solution.py:309

commit v3 on v2

--- a/solution.py
+++ b/solution.py
@@ -10,10 +10,13 @@
 RING = 8
 SIZES = (2048,) * 4
 CHUNKS = len(SIZES)
-STAGGER, STEP, CROSS = 0.6, 1.0, 4.0
+STAGGER, STEP, CROSS, SPREAD = 0.6, 1.0, 4.0, 0.6
 BLOCK = 16
 LIMIT = 1e30
+RELAY = 1.6
 FIRST = 3
+RELAYED = (0,)
+RUN = 12
 BITS = (2, 4, 8)
 LOWEST = (-8, -9, -12)
 
@@ -29,11 +32,14 @@
         for s in range(1, 5):
             steps.append((begin + step * (s - 1), 0, ("reduce", c, s)))
         done = begin + step * 4
+        ready = step * 4 + cross + SPREAD * c
         steps.append((done, 0, ("finish", c, 0)))
-        steps.append((done + cross, 1, ("hidden", c, 0)))
+        steps.append((ready, 1, ("hidden", c, 0)))
+        if c in RELAYED:
+            steps.append((done + RELAY, 0, ("relay", c, 0)))
         for s in range(1, 4):
-            steps.append((done + cross + step * s, 1, ("gather", c, s)))
-        steps.append((done + cross + step * 4.5, 2, ("product", c, 0)))
+            steps.append((ready + step * s, 1, ("gather", c, s)))
+        steps.append((ready + step * 4.5, 2, ("product", c, 0)))
         steps.append((1.5 + 0.7 * c, 3, ("mix", c, 0)))
     steps.sort(key=lambda item: item[:2])
     return [item[2] for item in steps]
@@ -45,6 +51,7 @@
     powers, logits, counts, gain, taken, product_out,
     terms, residual, weight, mixed, arrived, partial, crossed, gathered, scaled, total, squares,
     load_sem, term_sem, store_sem, reduce_send, reduce_recv, cross_send, cross_recv, gather_send, gather_recv,
+    relayed, relay_send, relay_recv,
 ):
     f32, bf16 = jnp.float32, jnp.bfloat16
     section, sections = lax.axis_index("segment"), lax.axis_size("segment")
@@ -54,6 +61,20 @@
     neighbour = (ring + lax.rem(y + 1, RING), ring + lax.rem(y + RING - 1, RING))
     far = lax.rem(t + RING, 2 * RING)
     after, before = lax.rem(section + 1, sections), lax.rem(section + sections - 1, sections)
+    place = lax.rem(section, RUN)
+    spot = lax.div(place, 2)
+    first_core = lax.rem(place, 2) == 0
+    by_relay = jnp.logical_and(lax.rem(spot, 2) == 1, first_core)
+    is_relay = jnp.logical_and(lax.rem(spot, 2) == 0, first_core)
+    last_spot = RUN // 2 - 1
+    wrapped = lax.div(spot, last_spot)
+    relay_at = (section - place + lax.rem(place + 2, RUN), lax.rem(t + RING * wrapped, 2 * RING))
+    wraps = lax.div(last_spot - spot, last_spot)
+    relay_source = (section - place + lax.rem(place + RUN - 2, RUN), lax.rem(t + RING * wraps, 2 * RING))
+    relay_target = (section - place + lax.rem(place + RUN - 1, RUN), lax.rem(t + RING + RING * wraps, 2 * RING))
+    is_target = jnp.logical_and(lax.rem(spot, 2) == 1, lax.rem(place, 2) == 1)
+    relay_from = (section - place + lax.rem(place + 1, RUN), lax.rem(t + RING + RING * wrapped, 2 * RING))
+
     depth = terms.shape[1]
     starts = [sum(SIZES[:c]) for c in range(CHUNKS)]
 
@@ -71,6 +92,14 @@
         pl.semaphore_signal(barrier, inc=1, device_id=(section, there), device_id_type=MESH)
     for there in (t, far):
         pl.semaphore_signal(barrier, inc=1, device_id=(before, there), device_id_type=MESH)
+
+    @pl.when(is_relay)
+    def _():
+        pl.semaphore_signal(barrier, inc=1, device_id=relay_source, device_id_type=MESH)
+
+    @pl.when(is_target)
+    def _():
+        pl.semaphore_signal(barrier, inc=1, device_id=relay_from, device_id_type=MESH)
 
     loads = [
         pltpu.make_async_copy(src, dst, load_sem.at[i])
@@ -142,14 +171,36 @@
             receive(src, reduce_recv.at[direction, last, c])
             value = value + src[...].astype(f32)
         partial[:, columns(c)] = value.astype(bf16)
-        for slot, there in ((1, far), (0, t)):
-            send(
-                partial.at[:, columns(c)],
-                crossed.at[slot, :, columns(c)],
-                cross_send.at[slot, c],
-                cross_recv.at[slot, c],
-                (after, there),
+        def across(dst, recv_sem, there):
+            return pltpu.make_async_remote_copy(
+                src_ref=partial.at[:, columns(c)], dst_ref=dst, send_sem=cross_send.at[1, c], recv_sem=recv_sem,
+                device_id=there, device_id_type=MESH,
             )
+
+        direct = across(crossed.at[1, :, columns(c)], cross_recv.at[1, c], (after, far))
+        if c in RELAYED:
+            pl.when(by_relay)(across(relayed.at[:, columns(c)], relay_recv.at[c], relay_at).start)
+            pl.when(jnp.logical_not(by_relay))(direct.start)
+        else:
+            direct.start()
+        sent.append(direct)
+        send(
+            partial.at[:, columns(c)], crossed.at[0, :, columns(c)], cross_send.at[0, c], cross_recv.at[0, c],
+            (after, t),
+        )
+
+    def passing(c):
+        return pltpu.make_async_remote_copy(
+            src_ref=relayed.at[:, columns(c)], dst_ref=crossed.at[1, :, columns(c)],
+            send_sem=relay_send.at[c], recv_sem=cross_recv.at[1, c],
+            device_id=relay_target, device_id_type=MESH,
+        )
+
+    def relay(c, s):
+        @pl.when(is_relay)
+        def _():
+            receive(relayed.at[:, columns(c)], relay_recv.at[c])
+            passing(c).start()
 
     def pass_on(c, s, d):
         for direction in range(2):
@@ -221,7 +272,7 @@
         lax.fori_loop(0, tiles, one, 0)
 
     join(0, 0)
-    pl.semaphore_wait(barrier, 4)
+    pl.semaphore_wait(barrier, 5 - lax.rem(place, 2))
     reduce(0, 1)
     for c in range(1, CHUNKS):
         join(c, 0)
@@ -238,7 +289,7 @@
 
     order = [x for x in schedule(CHUNKS) if x[0] != "reduce" or x[2] > 1 or x[1] >= FIRST]
     first_product = [c for name, c, s in order if name == "product"][0]
-    act = dict(reduce=reduce, finish=finish, hidden=hidden, gather=gather, product=product, mix=mix)
+    act = dict(reduce=reduce, finish=finish, hidden=hidden, relay=relay, gather=gather, product=product, mix=mix)
     for name, c, s in order:
         act[name](c, s)
 
@@ -250,6 +301,11 @@
         copy.wait_send()
     for copy in stores:
         copy.wait()
+
+    @pl.when(is_relay)
+    def _():
+        for c in RELAYED:
+            passing(c).wait_send()
 
 
 def hand_out(stream_in, product_in, stream, key_values):
@@ -301,6 +357,9 @@
             dma((2, CHUNKS)),
             dma((2, 4, CHUNKS)),
             dma((2, 4, CHUNKS)),
+            vmem((BLOCK, depth), bf16),
+            dma((CHUNKS,)),
+            dma((CHUNKS,)),
         ],
         compiler_params=pltpu.CompilerParams(
             collective_id=0, has_side_effects=True, vmem_limit_bytes=56 << 20

time: 76.6 us -> 74.5 us (0.973)
  the two profiles are of different devices: /device:TPU:69 before, /device:TPU:6 now
where the time goes in v3:
time: 74.5 us; the launch traced here: 73.3 us
  Pallas kernels  72.7 us (98%)
    pallas_call x1, Pallas kernels, body(): pl.pallas_call(kernel, out_shape=out_shape, in_specs=[pl.BlockSpec(memory...  71.1 us
    pallas_call x1, Pallas kernels, body(): pl.pallas_call(hand_out, out_shape=out_shape, in_specs=[pl.BlockSpec(memo...  1.57 us

profile of v3, /device:TPU:6, one launch (start us, length us, event | category | flops | bytes accessed | tf_op | source)
XLA Modules:
  0.0 73.3 jit_solution(11552330075341715414)
XLA Ops:
  0.6 71.1 %shard_map.86 = (bf16[8,8192]{1,0:T(8,128)(2,1)}, bf16[128,128]{1,0:T(8,128)(2,1)}) custom-call(s32[3,1,1,64]{3,2,1,0:T(1,128)} %bitcast.7, f32[3,80]{1,0:T(4,128)} %bitcast.6, s32[48]{0:T(128)} %counts_hbm.1, bf16[128,8192]{1,0:T(8,128)(2,1)} %bitcast.4, bf16[8,8192]{1,0:T(8,128)(2,1)} %residual_hbm.1, bf16[1,8192]{1,0:T(2,128)(2,1)} %gain_hbm.1, ...), custom_call_target="tpu_custom_call" | custom-call | tf_op jit(solution)/shard_map/pallas_call | solution.py:328
  71.7 1.6 %shard_map.87 = (bf16[8,8192]{1,0:T(8,128)(2,1)}, bf16[128,128]{1,0:T(8,128)(2,1)}) custom-call(bf16[8,8192]{1,0:T(8,128)(2,1)} %get-tuple-element.4.stream_in, bf16[128,128]{1,0:T(8,128)(2,1)} %get-tuple-element.5.product_in), custom_call_target="tpu_custom_call" | custom-call | tf_op jit(solution)/shard_map/pallas_call | solution.py:368

commit v4 on v3

--- a/solution.py
+++ b/solution.py
@@ -10,7 +10,7 @@
 RING = 8
 SIZES = (2048,) * 4
 CHUNKS = len(SIZES)
-STAGGER, STEP, CROSS, SPREAD = 0.6, 1.0, 4.0, 0.6
+STAGGER, STEP, CROSS, SPREAD = 0.75, 1.0, 4.0, 0.6
 BLOCK = 16
 LIMIT = 1e30
 RELAY = 1.6

time: 74.5 us -> 72.9 us (0.979)
  Pallas kernels: 72.7 us -> 71 us
    pallas_call x1, Pallas kernels: 71.1 us -> 69.4 us  [body(): pl.pallas_call(kernel, out_shape=out_shape, in_specs=[pl.BlockSpec(memory...]
where the time goes in v4:
time: 72.9 us; the launch traced here: 71.6 us
  Pallas kernels  71 us (97%)
    pallas_call x1, Pallas kernels, body(): pl.pallas_call(kernel, out_shape=out_shape, in_specs=[pl.BlockSpec(memory...  69.4 us
    pallas_call x1, Pallas kernels, body(): pl.pallas_call(hand_out, out_shape=out_shape, in_specs=[pl.BlockSpec(memo...  1.57 us

profile of v4, /device:TPU:6, one launch (start us, length us, event | category | flops | bytes accessed | tf_op | source)
XLA Modules:
  0.0 71.6 jit_solution(16197235131573499076)
XLA Ops:
  0.6 69.4 %shard_map.86 = (bf16[8,8192]{1,0:T(8,128)(2,1)}, bf16[128,128]{1,0:T(8,128)(2,1)}) custom-call(s32[3,1,1,64]{3,2,1,0:T(1,128)} %bitcast.7, f32[3,80]{1,0:T(4,128)} %bitcast.6, s32[48]{0:T(128)} %counts_hbm.1, bf16[128,8192]{1,0:T(8,128)(2,1)} %bitcast.4, bf16[8,8192]{1,0:T(8,128)(2,1)} %residual_hbm.1, bf16[1,8192]{1,0:T(2,128)(2,1)} %gain_hbm.1, ...), custom_call_target="tpu_custom_call" | custom-call | tf_op jit(solution)/shard_map/pallas_call | solution.py:328
  70.1 1.6 %shard_map.87 = (bf16[8,8192]{1,0:T(8,128)(2,1)}, bf16[128,128]{1,0:T(8,128)(2,1)}) custom-call(bf16[8,8192]{1,0:T(8,128)(2,1)} %get-tuple-element.4.stream_in, bf16[128,128]{1,0:T(8,128)(2,1)} %get-tuple-element.5.product_in), custom_call_target="tpu_custom_call" | custom-call | tf_op jit(solution)/shard_map/pallas_call | solution.py:368

commit v5 on v4

--- a/solution.py
+++ b/solution.py
@@ -39,7 +39,7 @@
             steps.append((done + RELAY, 0, ("relay", c, 0)))
         for s in range(1, 4):
             steps.append((ready + step * s, 1, ("gather", c, s)))
-        steps.append((ready + step * 4.5, 2, ("product", c, 0)))
+        steps.append((ready + step * 4.9, 2, ("product", c, 0)))
         steps.append((1.5 + 0.7 * c, 3, ("mix", c, 0)))
     steps.sort(key=lambda item: item[:2])
     return [item[2] for item in steps]

time: 72.9 us -> 72.9 us (level)
  no operation moved by 1% of the time
where the time goes in v5:
time: 72.9 us; the launch traced here: 71.6 us
  Pallas kernels  71 us (97%)
    pallas_call x1, Pallas kernels, body(): pl.pallas_call(kernel, out_shape=out_shape, in_specs=[pl.BlockSpec(memory...  69.4 us
    pallas_call x1, Pallas kernels, body(): pl.pallas_call(hand_out, out_shape=out_shape, in_specs=[pl.BlockSpec(memo...  1.57 us

profile of v5, /device:TPU:6, one launch (start us, length us, event | category | flops | bytes accessed | tf_op | source)
XLA Modules:
  0.0 71.6 jit_solution(4515287999000324376)
XLA Ops:
  0.6 69.4 %shard_map.86 = (bf16[8,8192]{1,0:T(8,128)(2,1)}, bf16[128,128]{1,0:T(8,128)(2,1)}) custom-call(s32[3,1,1,64]{3,2,1,0:T(1,128)} %bitcast.7, f32[3,80]{1,0:T(4,128)} %bitcast.6, s32[48]{0:T(128)} %counts_hbm.1, bf16[128,8192]{1,0:T(8,128)(2,1)} %bitcast.4, bf16[8,8192]{1,0:T(8,128)(2,1)} %residual_hbm.1, bf16[1,8192]{1,0:T(2,128)(2,1)} %gain_hbm.1, ...), custom_call_target="tpu_custom_call" | custom-call | tf_op jit(solution)/shard_map/pallas_call | solution.py:328
  70.1 1.6 %shard_map.87 = (bf16[8,8192]{1,0:T(8,128)(2,1)}, bf16[128,128]{1,0:T(8,128)(2,1)}) custom-call(bf16[8,8192]{1,0:T(8,128)(2,1)} %get-tuple-element.4.stream_in, bf16[128,128]{1,0:T(8,128)(2,1)} %get-tuple-element.5.product_in), custom_call_target="tpu_custom_call" | custom-call | tf_op jit(solution)/shard_map/pallas_call | solution.py:368
